TPU v7x, 32 devices: a whole 2x2x4 slice. The times are simulated.
32 devices in a mesh: dp: 4 (over y, x), expert: 8 (over z, core).
Axes of the slice: x: 2, y: 2, z: 4, core: 2. Of those that a mesh axis runs over, the one named last changes fastest.
Arguments:
- tokens: bfloat16 [768, 7168], P(('dp', 'expert')), may hold values from -6 to 6
- grad_out: bfloat16 [768, 7168], P(('dp', 'expert')), may hold values from -6 to 6
- route_ids: int32 [768, 8], P(('dp', 'expert')), may hold values from 0 to 31, all different within a row; in each aligned block of 24 rows (0 to 23, 24 to 47, ...) at most 7 rows name the same one
- route_weight: bfloat16 [768, 8], P(('dp', 'expert')), may hold values from 0.049804688 to 1
- cluster_of: int32 [32], replicated, may hold values from 0 to 3, as said below
- gate_basis: bfloat16 [4, 512, 7168], P(None, 'expert', 'dp'), may hold values from -0.0625 to 0.0625
- up_basis: bfloat16 [4, 512, 7168], P(None, 'expert', 'dp'), may hold values from -0.0625 to 0.0625
- down_basis: bfloat16 [4, 512, 7168], P(None, 'expert', 'dp'), may hold values from -0.25 to 0.25
- gate_factor: bfloat16 [32, 512, 2048], P('expert', None, 'dp'), may hold values from -0.25 to 0.25
- up_factor: bfloat16 [32, 512, 2048], P('expert', None, 'dp'), may hold values from -0.25 to 0.25
- down_factor: bfloat16 [32, 2048, 512], P('expert', 'dp'), may hold values from -0.125 to 0.125
Outputs:
- grad_tokens: bfloat16 [768, 7168], P(('dp', 'expert'))
- grad_route: float32 [768, 8], P(('dp', 'expert'))
- grad_gate_basis: float32 [4, 512, 7168], P(None, 'expert', 'dp')
- grad_up_basis: float32 [4, 512, 7168], P(None, 'expert', 'dp')
- grad_down_basis: float32 [4, 512, 7168], P(None, 'expert', 'dp')
- grad_gate_factor: float32 [32, 512, 2048], P('expert', None, 'dp')
- grad_up_factor: float32 [32, 512, 2048], P('expert', None, 'dp')
- grad_down_factor: float32 [32, 2048, 512], P('expert', 'dp')
Inputs may be any that keep to these rules, and one draw needn't show every extreme that they name: `route_ids`: each token names 8 different experts. Among the 24 tokens of one block no expert is named more than 7 times, and in every draw some expert is named exactly 7 times in some block. `cluster_of`: never falls from one expert to the next; all 4 experts of each group of 4 consecutive experts share one cluster; every cluster holds 1 to 3 such groups, and one holds exactly 3.
All inputs are finite; a program needn't handle non-finite values.
Results may differ from a plain program's by a relative error of at most 0.013.
Values may be sent and summed in bfloat16 or wider, within the bound.
No kernel may reach another device: no remote copies, remote signals or barrier semaphores. Data moves between devices by JAX's collectives and lax.ppermute only.
A program may use at most 128 MiB of HBM per device.

v0:
```python
import jax
import jax.numpy as jnp
from jax import lax
from jax.sharding import PartitionSpec as P


def silu_pair(pre):
    sig = jax.nn.sigmoid(pre)
    return (pre * sig, sig * (1.0 + pre * (1.0 - sig)))


def dp_total(terms):
    return lax.psum(terms, "dp")


def body(
    tokens,
    grad_out,
    route_ids,
    route_weight,
    cluster_of,
    gate_basis,
    up_basis,
    down_basis,
    gate_factor,
    up_factor,
    down_factor,
):
    fl = jnp.float32
    bf = jnp.bfloat16
    n_dp = lax.axis_size("dp")
    n_ex = lax.axis_size("expert")
    tok_rows, model_width = tokens.shape
    top_count = route_ids.shape[1]
    local_count = gate_factor.shape[0]
    experts = local_count * n_ex
    capacity = max(2, 5 * tok_rows * top_count // (4 * experts))
    slice_width = model_width // n_dp
    slot_cells = experts * capacity
    lane_rows = local_count * capacity
    sources = n_dp * n_ex
    total_rows = sources * lane_rows
    clusters = gate_basis.shape[0]
    rank = gate_factor.shape[1]
    flat_ids = route_ids.reshape(-1)
    matches = (flat_ids[:, None] == jnp.arange(experts, dtype=jnp.int32)[None, :]).astype(jnp.int32)
    slot_rank = jnp.sum(matches * jnp.cumsum(matches, axis=0), axis=1) - 1
    target = (flat_ids * capacity + slot_rank).reshape(tok_rows, top_count)
    placed = target[None, :, :] == jnp.arange(slot_cells, dtype=jnp.int32)[:, None, None]
    spread = jnp.any(placed, axis=2).astype(bf)
    slot_weight = jnp.sum(
        jnp.where(placed, route_weight[None].astype(fl), 0.0), axis=(1, 2)
    ).astype(bf)
    send_x = (
        jnp.einsum(
            "ct,tqf->qcf",
            spread,
            tokens.reshape(tok_rows, n_dp, slice_width),
            preferred_element_type=fl,
        )
        .astype(bf)
        .reshape(n_dp, n_ex, lane_rows, slice_width)
    )
    send_dy = (
        jnp.einsum(
            "ct,tqf->qcf",
            spread,
            grad_out.reshape(tok_rows, n_dp, slice_width),
            preferred_element_type=fl,
        )
        .astype(bf)
        .reshape(n_dp, n_ex, lane_rows, slice_width)
    )
    send_w = jnp.broadcast_to(slot_weight.reshape(1, n_ex, lane_rows), (n_dp, n_ex, lane_rows))
    got_x, got_dy, got_w = (
        lax.all_to_all(
            send_x.reshape(sources, lane_rows, slice_width),
            ("dp", "expert"),
            split_axis=0,
            concat_axis=0,
            tiled=True,
        ),
        lax.all_to_all(
            send_dy.reshape(sources, lane_rows, slice_width),
            ("dp", "expert"),
            split_axis=0,
            concat_axis=0,
            tiled=True,
        ),
        lax.all_to_all(
            send_w.reshape(sources, lane_rows),
            ("dp", "expert"),
            split_axis=0,
            concat_axis=0,
            tiled=True,
        ),
    )
    x_rows = got_x.reshape(total_rows, slice_width)
    dy_rows = got_dy.reshape(total_rows, slice_width)
    weight_rows = got_w.reshape(total_rows)
    group_cluster = cluster_of.reshape(n_ex, local_count)[:, 0]
    pick_table = (group_cluster[:, None] == jnp.arange(clusters, dtype=jnp.int32)[None, :]).astype(
        bf
    )
    stacked = jnp.stack([gate_basis, up_basis, down_basis])
    outgoing = jnp.einsum("jc,bcrf->jbrf", pick_table, stacked, preferred_element_type=fl).astype(
        bf
    )
    basis_rows = lax.all_to_all(outgoing, "expert", split_axis=0, concat_axis=2, tiled=True)
    gate_rows = basis_rows[0, 0]
    up_rows = basis_rows[0, 1]
    down_rows = basis_rows[0, 2]
    shape_four = (sources, local_count, capacity, rank)
    first_sums = dp_total(
        (
            jnp.einsum("nf,rf->nr", x_rows, gate_rows, preferred_element_type=fl),
            jnp.einsum("nf,rf->nr", x_rows, up_rows, preferred_element_type=fl),
        )
    )
    rank_gate = first_sums[0].astype(bf).reshape(shape_four)
    rank_up = first_sums[1].astype(bf).reshape(shape_four)
    gate_pre = jnp.einsum("sekr,erf->sekf", rank_gate, gate_factor, preferred_element_type=fl)
    up_pre = jnp.einsum("sekr,erf->sekf", rank_up, up_factor, preferred_element_type=fl)
    act, slope = silu_pair(gate_pre)
    hidden = (act * up_pre).astype(bf)
    mixed_sum = dp_total(
        (jnp.einsum("sekf,efr->sekr", hidden, down_factor, preferred_element_type=fl),)
    )
    mixed = mixed_sum[0].astype(bf).reshape(total_rows, rank)
    y_rows = jnp.dot(mixed, down_rows, preferred_element_type=fl)
    partial_dots = jnp.sum(y_rows * dy_rows.astype(fl), axis=1)
    upstream = (weight_rows[:, None].astype(fl) * dy_rows.astype(fl)).astype(bf)
    term_down = jnp.einsum("nr,nf->rf", mixed, upstream, preferred_element_type=fl)
    mixed_back = dp_total(
        (jnp.einsum("nf,rf->nr", upstream, down_rows, preferred_element_type=fl),)
    )
    grad_mixed = mixed_back[0].astype(bf).reshape(shape_four)
    grad_down_factor = jnp.einsum("sekf,sekr->efr", hidden, grad_mixed, preferred_element_type=fl)
    grad_hidden = jnp.einsum("sekr,efr->sekf", grad_mixed, down_factor, preferred_element_type=fl)
    grad_gate_pre = (grad_hidden * up_pre * slope).astype(bf)
    grad_up_pre = (grad_hidden * act).astype(bf)
    grad_gate_factor = jnp.einsum(
        "sekr,sekf->erf", rank_gate, grad_gate_pre, preferred_element_type=fl
    )
    grad_up_factor = jnp.einsum("sekr,sekf->erf", rank_up, grad_up_pre, preferred_element_type=fl)
    rank_back = dp_total(
        (
            jnp.einsum("sekf,erf->sekr", grad_gate_pre, gate_factor, preferred_element_type=fl),
            jnp.einsum("sekf,erf->sekr", grad_up_pre, up_factor, preferred_element_type=fl),
        )
    )
    grad_hg = rank_back[0].astype(bf).reshape(total_rows, rank)
    grad_hu = rank_back[1].astype(bf).reshape(total_rows, rank)
    term_gate = jnp.einsum("nr,nf->rf", grad_hg, x_rows, preferred_element_type=fl)
    term_up = jnp.einsum("nr,nf->rf", grad_hu, x_rows, preferred_element_type=fl)
    grad_x = (
        jnp.dot(grad_hg, gate_rows, preferred_element_type=fl)
        + jnp.dot(grad_hu, up_rows, preferred_element_type=fl)
    ).astype(bf)
    group_terms = jnp.stack([term_gate, term_up, term_down]).astype(bf)[None]
    gathered_terms = lax.all_to_all(group_terms, "expert", split_axis=2, concat_axis=0, tiled=True)
    cluster_grads = jnp.einsum(
        "jc,jbrf->cbrf", pick_table, gathered_terms, preferred_element_type=fl
    )
    returned = lax.all_to_all(
        grad_x.reshape(sources, lane_rows, slice_width),
        ("dp", "expert"),
        split_axis=0,
        concat_axis=0,
        tiled=True,
    )
    returned_dots = lax.all_to_all(
        partial_dots.reshape(sources, lane_rows),
        ("dp", "expert"),
        split_axis=0,
        concat_axis=0,
        tiled=True,
    )
    returned = returned.reshape(n_dp, slot_cells, slice_width)
    cell_scores = jnp.sum(returned_dots.reshape(n_dp, slot_cells), axis=0)
    grad_tokens = (
        jnp.einsum("ct,qcf->tqf", spread, returned, preferred_element_type=fl)
        .reshape(tok_rows, model_width)
        .astype(bf)
    )
    grad_route = jnp.sum(jnp.where(placed, cell_scores[:, None, None], 0.0), axis=0)
    return (
        grad_tokens,
        grad_route,
        cluster_grads[:, 0],
        cluster_grads[:, 1],
        cluster_grads[:, 2],
        grad_gate_factor,
        grad_up_factor,
        grad_down_factor,
    )


def solution(mesh):
    in_specs = (
        P(("dp", "expert"), None),
        P(("dp", "expert"), None),
        P(("dp", "expert"), None),
        P(("dp", "expert"), None),
        P(),
        P(None, "expert", "dp"),
        P(None, "expert", "dp"),
        P(None, "expert", "dp"),
        P("expert", None, "dp"),
        P("expert", None, "dp"),
        P("expert", "dp", None),
    )
    out_specs = (
        P(("dp", "expert"), None),
        P(("dp", "expert"), None),
        P(None, "expert", "dp"),
        P(None, "expert", "dp"),
        P(None, "expert", "dp"),
        P("expert", None, "dp"),
        P("expert", None, "dp"),
        P("expert", "dp", None),
    )
    return jax.shard_map(body, mesh=mesh, in_specs=in_specs, out_specs=out_specs, check_vma=False)
```

profile of v0, /device:TPU:0, one launch (start us, length us, event | category | flops | bytes accessed | tf_op | source)
XLA Modules:
  0.0 1067.6 jit_solution(13250876524622443789)
XLA Ops:
  6.6 5.4 reshape_reshape.7
  12.0 7.4 all-to-all-start.3
  22.1 5.4 reshape_reshape.6
  27.6 75.7 %all-to-all-done.3 = bf16[32,28,1792]{2,1,0:T(8,128)(2,1)} async-done(((bf16[32,28,1792]{2,1,0:T(8,128)(2,1)}), bf16[32,28,1792]{2,1,0:T(8,128)(2,1)}, u32[]{:S(2)}, u32[]{:S(2)}) %all-to-all-start.3) | async-done | bytes 3211296 | tf_op jit(solution)/shard_map/all_to_all | solution.py:76
  118.3 72.4 %all-to-all-done.1 = bf16[32,28,1792]{2,1,0:T(8,128)(2,1)} async-done(((bf16[32,28,1792]{2,1,0:T(8,128)(2,1)}), bf16[32,28,1792]{2,1,0:T(8,128)(2,1)}, u32[]{:S(2)}, u32[]{:S(2)}) %all-to-all-start.1) | async-done | bytes 3211296 | tf_op jit(solution)/shard_map/all_to_all | solution.py:83
  195.3 5.5 reshape.177
  200.8 6.0 reshape.188
  206.8 110.7 %all-to-all-done.2 = bf16[8,3,64,1792]{3,2,1,0:T(8,128)(2,1)} async-done(((bf16[8,3,64,1792]{3,2,1,0:T(8,128)(2,1)}), bf16[8,3,64,1792]{3,2,1,0:T(8,128)(2,1)}, u32[]{:S(2)}, u32[]{:S(2)}) %all-to-all-start.2) | async-done | bytes 5505056 | tf_op jit(solution)/shard_map/all_to_all | solution.py:109
  327.1 126.2 %all-reduce.7 = (bf16[896,512]{1,0:T(8,128)(2,1)}, bf16[896,512]{1,0:T(8,128)(2,1)}) all-reduce(f32[896,512]{1,0:T(8,128)} %fusion.37, f32[896,512]{1,0:T(8,128)} %fusion.35), channel_id=1, replica_groups=mesh['dp'=4,'expert'=8] {'dp'}, use_global_device_ids=true, to_apply=%region_7.8 | all-reduce | flops 917504 | bytes 5505024 | tf_op jit(solution)/shard_map/psum | solution.py:13
  465.3 64.2 %all-reduce.8 = bf16[32,4,7,512]{3,0,2,1:T(8,128)(2,1)} all-reduce(f32[32,4,7,512]{3,0,2,1:T(8,128)} %fusion.41), channel_id=1, replica_groups=mesh['dp'=4,'expert'=8] {'dp'}, use_global_device_ids=true, to_apply=%region_10.11 | all-reduce | flops 458752 | bytes 2752512 | tf_op jit(solution)/shard_map/psum | solution.py:13
  532.4 5.6 multiply_reduce_fusion
  543.5 7.0 all-to-all-done.5
  552.0 8.8 all_to_all.69
  565.5 5.4 convert_element_type.112
  570.9 5.5 fusion.34
  576.4 66.1 %all-reduce.9 = bf16[896,512]{1,0:T(8,128)(2,1)S(1)} all-reduce(f32[896,512]{1,0:T(8,128)} %fusion.34), channel_id=1, replica_groups=mesh['dp'=4,'expert'=8] {'dp'}, use_global_device_ids=true, to_apply=%region_5.6 | all-reduce | flops 458752 | bytes 2752512 | tf_op jit(solution)/shard_map/psum | solution.py:13
  651.8 124.3 %all-reduce.10 = (bf16[32,4,7,512]{3,0,2,1:T(8,128)(2,1)}, bf16[32,4,7,512]{3,0,2,1:T(8,128)(2,1)}) all-reduce(f32[32,4,7,512]{3,0,2,1:T(8,128)S(1)} %fusion.44, f32[32,4,7,512]{3,0,2,1:T(8,128)} %fusion.38), channel_id=1, replica_groups=mesh['dp'=4,'expert'=8] {'dp'}, use_global_device_ids=true, to_apply=%region_8.9 | all-reduce | flops 917504 | bytes 5505024 | tf_op jit(solution)/shard_map/psum | solution.py:13
  778.1 6.4 fusion.36
  785.4 7.0 add_convert_fusion
  813.1 10.2 copy.139
  823.4 62.1 %all-to-all-done.4 = bf16[32,28,1792]{2,1,0:T(8,128)(2,1)} async-done(((bf16[32,28,1792]{2,1,0:T(8,128)(2,1)}), bf16[32,28,1792]{2,1,0:T(8,128)(2,1)}, u32[]{:S(2)}, u32[]{:S(2)}) %all-to-all-start.4) | async-done | bytes 3211296 | tf_op jit(solution)/shard_map/all_to_all | solution.py:165
  901.5 5.5 reshape.183
  910.5 141.5 %all-to-all-done.6 = bf16[1,3,512,1792]{3,1,0,2:T(4,128)(2,1)} async-done(((bf16[1,3,512,1792]{3,1,0,2:T(4,128)(2,1)}), bf16[1,3,512,1792]{3,1,0,2:T(4,128)(2,1)}, u32[]{:S(2)}, u32[]{:S(2)}) %all-to-all-start.6) | async-done | bytes 5505056 | tf_op jit(solution)/shard_map/all_to_all | solution.py:161
  1052.0 9.5 fusion
  (124 shorter events, 122.4 us)
Async XLA Ops:
  0.6 462.8 %copy-start = (bf16[4,512,512]{2,1,0:T(8,128)(2,1)S(1)}, bf16[4,512,512]{2,1,0:T(8,128)(2,1)}, u32[]{:S(2)}) copy-start(bf16[4,512,512]{2,1,0:T(8,128)(2,1)} %param.21) | copy-start | bytes 6291460
  12.0 7.4 copy-start.23
  12.0 91.3 %all-to-all-start.3 = ((bf16[32,28,1792]{2,1,0:T(8,128)(2,1)}), bf16[32,28,1792]{2,1,0:T(8,128)(2,1)}, u32[]{:S(2)}, u32[]{:S(2)}) async-start(bf16[32,28,1792]{2,1,0:T(8,128)(2,1)} %reshape_reshape.7), calls=%async_computation.3 | async-start | bytes 7340032 | tf_op jit(solution)/shard_map/all_to_all | solution.py:76
  27.6 82.1 %copy-start.25 = (s32[32]{0:T(128)S(1)}, s32[32]{0:T(128)}, u32[]{:S(2)}) copy-start(s32[32]{0:T(128)} %param.15) | copy-start | bytes 388
  27.6 82.3 %copy-start.14 = (bf16[4,64,1792]{2,1,0:T(8,128)(2,1)S(1)}, bf16[4,64,1792]{2,1,0:T(8,128)(2,1)}, u32[]{:S(2)}) copy-start(bf16[4,64,1792]{2,1,0:T(8,128)(2,1)} %param.18) | copy-start | bytes 2752516
  103.3 87.4 %all-to-all-start.1 = ((bf16[32,28,1792]{2,1,0:T(8,128)(2,1)}), bf16[32,28,1792]{2,1,0:T(8,128)(2,1)}, u32[]{:S(2)}, u32[]{:S(2)}) async-start(bf16[32,28,1792]{2,1,0:T(8,128)(2,1)} %reshape_reshape.6), calls=%async_computation.1 | async-start | bytes 7340032 | tf_op jit(solution)/shard_map/all_to_all | solution.py:83
  190.7 126.8 %all-to-all-start.2 = ((bf16[8,3,64,1792]{3,2,1,0:T(8,128)(2,1)}), bf16[8,3,64,1792]{3,2,1,0:T(8,128)(2,1)}, u32[]{:S(2)}, u32[]{:S(2)}) async-start(bf16[8,3,64,1792]{3,2,1,0:T(8,128)(2,1)} %copy.128), calls=%async_computation.2 | async-start | bytes 11010048 | tf_op jit(solution)/shard_map/all_to_all | solution.py:109
  317.4 3.5 copy-start.6
  320.7 3.4 copy-start.2
  454.7 5.3 copy-start.4
  532.4 11.0 %copy-start.24 = (bf16[24,8]{0,1:T(8,128)(2,1)S(1)}, bf16[24,8]{0,1:T(8,128)(2,1)}, u32[]{:S(2)}) copy-start(bf16[24,8]{0,1:T(8,128)(2,1)} %param.14) | copy-start | bytes 1156
  538.7 11.7 %all-to-all-start.5 = ((f32[32,1,28]{2,1,0:T(1,128)}), f32[32,1,28]{2,1,0:T(1,128)S(1)}, u32[]{:S(2)}, u32[]{:S(2)}) async-start(f32[32,1,28]{2,1,0:T(1,128)} %bitcast.34), calls=%async_computation.5 | async-start | bytes 32768 | tf_op jit(solution)/shard_map/all_to_all | solution.py:172
  643.8 4.1 copy-start.3
  778.1 6.4 copy-start.20
  778.1 6.4 copy-start.22
  797.7 3.9 copy-start.19
  797.7 87.7 %all-to-all-start.4 = ((bf16[32,28,1792]{2,1,0:T(8,128)(2,1)}), bf16[32,28,1792]{2,1,0:T(8,128)(2,1)}, u32[]{:S(2)}, u32[]{:S(2)}) async-start(bf16[32,28,1792]{2,1,0:T(8,128)(2,1)} %reshape.182), calls=%async_computation.4 | async-start | bytes 7340032 | tf_op jit(solution)/shard_map/all_to_all | solution.py:165
  801.6 4.2 copy-start.7
  823.4 67.8 %copy-start.5 = (bf16[32,4,7,512]{3,2,1,0:T(8,128)(2,1)S(1)}, bf16[32,4,7,512]{3,2,1,0:T(8,128)(2,1)}, u32[]{:S(2)}) copy-start(bf16[32,4,7,512]{3,2,1,0:T(8,128)(2,1)} %copy-done.4) | copy-start | bytes 2752516
  885.5 166.5 %all-to-all-start.6 = ((bf16[1,3,512,1792]{3,1,0,2:T(4,128)(2,1)}), bf16[1,3,512,1792]{3,1,0,2:T(4,128)(2,1)}, u32[]{:S(2)}, u32[]{:S(2)}) async-start(bf16[1,3,512,1792]{3,1,0,2:T(4,128)(2,1)} %copy.139), calls=%async_computation.6 | async-start | bytes 14680064 | tf_op jit(solution)/shard_map/all_to_all | solution.py:161
  891.2 4.2 copy-start.12
  895.5 3.0 copy-start.13
  895.5 3.0 copy-start.16
  1064.0 3.1 copy-start.1
  (8 other events, 16.6 us)
where the time goes:
time: 1080 us; the launch traced here: 1070 us
  waiting for transfers between devices  469 us (43%)
  blocking collectives  390 us (36%)
  local copies, waits for them, and re-layouts  86 us (8%)
  matrix products  82.5 us (8%)
  starting transfers between devices  29.3 us (3%)
    psum x4, blocking collectives, dp_total(): return lax.psum(terms, 'dp')  381 us
    all_to_all x1, waiting for transfers between devices, body(): lax.all_to_all(group_terms, 'expert', split_axis=2, concat_axis=0, tiled=...  141 us
    all_to_all x1, waiting for transfers between devices, body(): lax.all_to_all(outgoing, 'expert', split_axis=0, concat_axis=2, tiled=True)  111 us
    all_to_all x1, waiting for transfers between devices, body(): lax.all_to_all(send_x.reshape(sources, lane_rows, slice_width), ('dp', 'e...  75.7 us
    all_to_all x1, waiting for transfers between devices, body(): lax.all_to_all(send_dy.reshape(sources, lane_rows, slice_width), ('dp', '...  72.4 us
    all_to_all x1, waiting for transfers between devices, body(): lax.all_to_all(grad_x.reshape(sources, lane_rows, slice_width), ('dp', 'e...  62.1 us
  transfers between devices with their start and end apart: 6, of which 6 were waited for; matrix products, arithmetic and copies ran while one was open for 7% of the time, Pallas kernels for 0%

commit v1 on v0

v1 whole, which is shorter than its diff:
```python
import jax
import jax.numpy as jnp
from jax import lax
from jax.sharding import Mesh
from jax.sharding import PartitionSpec as P

FL = jnp.float32
BF = jnp.bfloat16


def silu_pair(pre):
    sig = jax.nn.sigmoid(pre)
    return (pre * sig, sig * (1.0 + pre * (1.0 - sig)))


def mm(spec, a, b):
    return jnp.einsum(spec, a, b, preferred_element_type=FL)


def core_swap(value):
    return lax.ppermute(value, "core", [(0, 1), (1, 0)])


def core_join(value):
    other = core_swap(value)
    first = lax.axis_index("core") == 0
    return jnp.stack([jnp.where(first, value, other), jnp.where(first, other, value)])


def gather_columns(rows, n_dp):
    tok_rows, width = rows.shape
    part = width // n_dp
    pieces = jnp.concatenate([rows[:, i * part : (i + 1) * part] for i in range(n_dp)], axis=0)
    pieces = lax.all_to_all(pieces, "dp", split_axis=0, concat_axis=0, tiled=True)
    along = lax.all_gather(pieces, "ez", axis=0, tiled=True)
    return core_join(along).reshape(-1, part)


def dp_scatter_sum(value):
    got = lax.all_to_all(value.astype(BF), "dp", split_axis=0, concat_axis=0, tiled=True)
    return jnp.sum(got.astype(FL), axis=0)


def body(
    tokens,
    grad_out,
    route_ids,
    route_weight,
    cluster_of,
    gate_basis,
    up_basis,
    down_basis,
    gate_factor,
    up_factor,
    down_factor,
):
    n_dp = lax.axis_size("dp")
    n_z = lax.axis_size("ez")
    n_ex = n_z * 2
    me_e = lax.axis_index("ez") * 2 + lax.axis_index("core")
    tok_rows, model_width = tokens.shape
    top = route_ids.shape[1]
    local = gate_factor.shape[0]
    experts = local * n_ex
    capacity = max(2, 5 * tok_rows * top // (4 * experts))
    blocks = n_dp * n_ex
    total = blocks * tok_rows
    slots = blocks * capacity
    clusters, rank_own, width = gate_basis.shape
    rank = gate_factor.shape[1]
    rank_part = rank_own // n_dp

    def everywhere(value):
        got = lax.all_gather(value, ("dp", "ez", "core"), axis=0, tiled=False)
        got = got.reshape(n_dp, n_z, 2, tok_rows, top)
        return got.transpose(2, 1, 0, 3, 4).reshape(blocks, tok_rows, top)

    ids = everywhere(route_ids)
    weights = everywhere(route_weight).astype(FL)
    own_ids = me_e * local + jnp.arange(local, dtype=jnp.int32)
    hit = ids[None] == own_ids[:, None, None, None]
    named = jnp.any(hit, axis=3)
    weight_of = jnp.sum(jnp.where(hit, weights[None], 0.0), axis=3)
    order = jnp.cumsum(named.astype(jnp.int32), axis=2) - 1
    cell = jnp.arange(blocks, dtype=jnp.int32)[None, :, None] * capacity + order
    cell = jnp.where(named, cell, -1).reshape(local, 1, total)
    placed = cell == jnp.arange(slots, dtype=jnp.int32)[None, :, None]
    weight_of = weight_of.reshape(local, 1, total)
    pick = placed.astype(BF).reshape(local * slots, total)
    pick_weighted = jnp.where(placed, weight_of, 0.0).astype(BF).reshape(local * slots, total)
    slot_weight = jnp.sum(jnp.where(placed, weight_of, 0.0), axis=2, keepdims=True)

    group_cluster = cluster_of.reshape(n_ex, local)[:, 0]

    def to_groups(rows, bases):
        count = len(bases)
        parts = [
            mm("rf,tf->rt", basis.reshape(clusters * rank_own, width), rows).reshape(
                clusters, n_dp, rank_part, total
            )
            for basis in bases
        ]
        terms = jnp.stack(parts)
        mine = dp_scatter_sum(terms.transpose(2, 0, 1, 3, 4)).astype(BF)
        send = jnp.take(mine, group_cluster, axis=1)
        send = send.transpose(1, 0, 2, 3)
        got = lax.all_to_all(send, ("ez", "core"), split_axis=0, concat_axis=0, tiled=True)
        full = lax.all_gather(got, "dp", axis=0, tiled=False)
        full = full.transpose(2, 1, 0, 3, 4).reshape(count, rank, total)
        return [full[i] for i in range(count)]

    x_cols = gather_columns(tokens, n_dp)
    dy_cols = gather_columns(grad_out, n_dp)
    hg_rows, hu_rows = to_groups(x_cols, [gate_basis, up_basis])
    (hd_rows,) = to_groups(dy_cols, [down_basis])

    def to_slots(rows):
        return mm("nt,rt->nr", pick, rows).astype(BF).reshape(local, slots, rank)

    hg = to_slots(hg_rows)
    hu = to_slots(hu_rows)
    hd = to_slots(hd_rows)
    gate_pre = mm("jnr,jrf->jnf", hg, gate_factor)
    up_pre = mm("jnr,jrf->jnf", hu, up_factor)
    act, slope = silu_pair(gate_pre)
    hidden = (act * up_pre).astype(BF)
    mixed = mm("jnf,jfr->jnr", hidden, down_factor)
    dots = jnp.sum(mixed * hd.astype(FL), axis=2, keepdims=True)
    grad_mixed = (slot_weight * hd.astype(FL)).astype(BF)
    grad_hidden = mm("jnr,jfr->jnf", grad_mixed, down_factor)
    grad_gate_pre = (grad_hidden * up_pre * slope).astype(BF)
    grad_up_pre = (grad_hidden * act).astype(BF)
    grad_down_factor = mm("jnf,jnr->jfr", hidden, grad_mixed)
    grad_gate_factor = mm("jnr,jnf->jrf", hg, grad_gate_pre)
    grad_up_factor = mm("jnr,jnf->jrf", hu, grad_up_pre)
    grad_hg = mm("jnf,jrf->jnr", grad_gate_pre, gate_factor).astype(BF)
    grad_hu = mm("jnf,jrf->jnr", grad_up_pre, up_factor).astype(BF)

    def from_groups(terms):
        count = len(terms)
        value = jnp.stack(terms).reshape(count, n_ex, n_dp, rank_part, total)
        mine = dp_scatter_sum(value.transpose(2, 1, 0, 3, 4)).astype(BF)
        got = lax.all_to_all(mine, ("ez", "core"), split_axis=0, concat_axis=0, tiled=True)
        owner = group_cluster[None, :] == jnp.arange(clusters, dtype=jnp.int32)[:, None]
        summed = jnp.sum(
            jnp.where(owner[:, :, None, None, None], got.astype(FL)[None], 0.0), axis=1
        ).astype(BF)
        full = lax.all_gather(summed, "dp", axis=0, tiled=False)
        full = full.transpose(2, 1, 0, 3, 4).reshape(count, clusters * rank_own, total)
        return [full[i] for i in range(count)]

    flat = lambda value: value.reshape(local * slots, rank)
    (sum_mixed,) = from_groups([mm("nr,nt->rt", flat(mixed.astype(BF)), pick_weighted)])
    sum_gate, sum_up = from_groups(
        [mm("nr,nt->rt", flat(grad_hg), pick), mm("nr,nt->rt", flat(grad_hu), pick)]
    )
    shape = (clusters, rank_own, width)
    grad_down_basis = mm("rt,tf->rf", sum_mixed, dy_cols).reshape(shape)
    grad_gate_basis = mm("rt,tf->rf", sum_gate, x_cols).reshape(shape)
    grad_up_basis = mm("rt,tf->rf", sum_up, x_cols).reshape(shape)

    grad_x = mm("rt,rf->tf", sum_gate, gate_basis.reshape(-1, width)) + mm(
        "rt,rf->tf", sum_up, up_basis.reshape(-1, width)
    )
    halves = grad_x.reshape(2, total // 2, width)
    core = lax.axis_index("core")
    keep = jnp.where(core == 0, halves[0], halves[1])
    give = jnp.where(core == 0, halves[1], halves[0]).astype(BF)
    half = (keep + core_swap(give).astype(FL)).astype(BF)
    got = lax.all_to_all(half, "ez", split_axis=0, concat_axis=0, tiled=True)
    mine = jnp.sum(got.reshape(n_z, n_dp * tok_rows, width).astype(FL), axis=0).astype(BF)
    mine = lax.all_to_all(mine, "dp", split_axis=0, concat_axis=0, tiled=True)
    grad_tokens = jnp.concatenate(
        [mine[i * tok_rows : (i + 1) * tok_rows] for i in range(n_dp)], axis=1
    )

    scores = jnp.sum(jnp.where(placed, dots, 0.0), axis=1)
    scores = scores.reshape(local, 2, n_z, n_dp, tok_rows).transpose(3, 2, 1, 0, 4)
    scores = scores.reshape(blocks, local, tok_rows)
    back = lax.all_to_all(scores, ("dp", "ez", "core"), split_axis=0, concat_axis=0, tiled=True)
    by_expert = jnp.sum(back.reshape(n_dp, experts, tok_rows), axis=0)
    chosen = route_ids[:, :, None] == jnp.arange(experts, dtype=jnp.int32)[None, None, :]
    grad_route = jnp.sum(jnp.where(chosen, by_expert.T[:, None, :], 0.0), axis=2)
    return (
        grad_tokens,
        grad_route,
        grad_gate_basis,
        grad_up_basis,
        grad_down_basis,
        grad_gate_factor,
        grad_up_factor,
        grad_down_factor,
    )


def solution(mesh):
    n_dp, n_ex = mesh.shape["dp"], mesh.shape["expert"]
    split = Mesh(mesh.devices.reshape(n_dp, n_ex // 2, 2), ("dp", "ez", "core"))
    ex = ("ez", "core")
    rows = P(("dp", "ez", "core"), None)
    basis = P(None, ex, "dp")
    in_specs = (
        rows,
        rows,
        rows,
        rows,
        P(),
        basis,
        basis,
        basis,
        P(ex, None, "dp"),
        P(ex, None, "dp"),
        P(ex, "dp", None),
    )
    out_specs = (
        rows,
        rows,
        basis,
        basis,
        basis,
        P(ex, None, "dp"),
        P(ex, None, "dp"),
        P(ex, "dp", None),
    )
    return jax.shard_map(body, mesh=split, in_specs=in_specs, out_specs=out_specs, check_vma=False)
```

time: 1080 us -> 435 us (0.40)
  waiting for transfers between devices: 469 us -> 130 us
  blocking collectives: 390 us -> 149 us
  local copies, waits for them, and re-layouts: 86 us -> 23.6 us
  matrix products: 82.5 us -> 45.2 us
  other arithmetic: 9.32 us -> 33.1 us
  between operations: 1.5 us -> 14.5 us
    all_to_all x6 -> x10, waiting for transfers between devices: 469 us -> 69.6 us  [the longest x3 21.4 us: dp_scatter_sum(): lax.all_to_all(value.astype(BF), 'dp', split_axis=0, concat_axis=0, tiled...]
    psum x4 -> x0, blocking collectives: 381 us -> none  [dp_total(): return lax.psum(terms, 'dp')]
    all_gather x0 -> x5, blocking collectives: none -> 108 us  [the longest x2 76.5 us: everywhere(): got = lax.all_gather(value, ('dp', 'ez', 'core'), axis=0, tiled=False)]
    all_gather x0 -> x3, waiting for transfers between devices: none -> 58.4 us  [the longest x2 58.4 us: gather_columns(): along = lax.all_gather(pieces, 'ez', axis=0, tiled=True)]
    dot_general x23 -> x21, matrix products: 82.5 us -> 45.2 us  [mm(): return jnp.einsum(spec, a, b, preferred_element_type=FL)]
    all_to_all x1 -> x3, blocking collectives: 8.84 us -> 40.4 us  [the longest x2 21.2 us: gather_columns(): lax.all_to_all(pieces, 'dp', split_axis=0, concat_axis=0, tiled=True)]
    another operation x5 -> x0, local copies, waits for them, and re-layouts: 23.7 us -> none  [the longest x1 10.2 us: body(): group_terms = jnp.stack([term_gate, term_up, term_down]).astype(bf)[None]]
    reshape x11 -> x4, local copies, waits for them, and re-layouts: 23.6 us -> 1.54 us  [the longest x1 0.67 us: body(): scores = scores.reshape(blocks, local, tok_rows)]
  transfers between devices with their start and end apart: 6 -> 16, of which waited for: 6 -> 12; matrix products, arithmetic and copies ran while one was open for 7% -> 12% of each run, Pallas kernels for 0% -> 0%
where the time goes in v1:
time: 435 us; the launch traced here: 433 us
  blocking collectives  149 us (34%)
  waiting for transfers between devices  130 us (30%)
  matrix products  45.2 us (10%)
  starting transfers between devices  37.5 us (9%)
  other arithmetic  33.1 us (8%)
  local copies, waits for them, and re-layouts  23.6 us (5%)
  between operations  14.5 us (3%)
    all_gather x2, blocking collectives, everywhere(): got = lax.all_gather(value, ('dp', 'ez', 'core'), axis=0, tiled=False)  76.5 us
    all_gather x2, waiting for transfers between devices, gather_columns(): along = lax.all_gather(pieces, 'ez', axis=0, tiled=True)  58.4 us
    dot_general x21, matrix products, mm(): return jnp.einsum(spec, a, b, preferred_element_type=FL)  45.2 us
    all_to_all x3, waiting for transfers between devices, dp_scatter_sum(): lax.all_to_all(value.astype(BF), 'dp', split_axis=0, concat_axis=0, tiled...  21.4 us
    all_to_all x2, blocking collectives, gather_columns(): lax.all_to_all(pieces, 'dp', split_axis=0, concat_axis=0, tiled=True)  21.2 us
    all_gather x2, blocking collectives, from_groups(): full = lax.all_gather(summed, 'dp', axis=0, tiled=False)  19.6 us
    all_to_all x1, blocking collectives, dp_scatter_sum(): lax.all_to_all(value.astype(BF), 'dp', split_axis=0, concat_axis=0, tiled...  19.2 us
    all_to_all x2, waiting for transfers between devices, to_groups(): lax.all_to_all(send, ('ez', 'core'), split_axis=0, concat_axis=0, tiled=T...  19.1 us
  transfers between devices with their start and end apart: 16, of which 12 were waited for; matrix products, arithmetic and copies ran while one was open for 12% of the time, Pallas kernels for 0%

profile of v1, /device:TPU:0, one launch (start us, length us, event | category | flops | bytes accessed | tf_op | source)
XLA Modules:
  0.0 433.2 jit_solution(3844115569941067643)
XLA Ops:
  8.5 11.8 %all_to_all.87 = bf16[4,24,1792]{2,1,0:T(8,128)(2,1)} all-to-all(bf16[4,24,1792]{2,1,0:T(8,128)(2,1)S(1)} %bitcast.177), channel_id=1, replica_groups=mesh['dp'=4,'ez'=4,'core'=2] {'dp'}, dimensions={0} | all-to-all | bytes 688128 | tf_op jit(solution)/shard_map/all_to_all | solution.py:34
  20.4 9.4 %all_to_all.88 = bf16[4,24,1792]{2,1,0:T(8,128)(2,1)} all-to-all(bf16[4,24,1792]{2,1,0:T(8,128)(2,1)S(1)} %bitcast.178), channel_id=1, replica_groups=mesh['dp'=4,'ez'=4,'core'=2] {'dp'}, dimensions={0} | all-to-all | bytes 688128 | tf_op jit(solution)/shard_map/all_to_all | solution.py:34
  29.8 24.1 %all-gather.14.cloned.1.call-done = bf16[384,1792]{1,0:T(8,128)(2,1)} async-done(((bf16[96,1792]{1,0:T(8,128)(2,1)}), bf16[384,1792]{1,0:T(8,128)(2,1)}) %all-gather.14.cloned.1.call-update) | async-done | bytes 1376272 | tf_op jit(solution)/shard_map/all_gather | solution.py:35
  53.9 34.4 %all-gather.12.cloned.1.call-done = bf16[384,1792]{1,0:T(8,128)(2,1)} async-done(((bf16[96,1792]{1,0:T(8,128)(2,1)}), bf16[384,1792]{1,0:T(8,128)(2,1)}) %all-gather.12.cloned.1.call-update) | async-done | bytes 1376272 | tf_op jit(solution)/shard_map/all_gather | solution.py:35
  100.0 4.2 all-to-all-start.4
  105.0 10.6 %all-to-all-done.4 = bf16[4,2,4,16,768]{4,3,2,1,0:T(8,128)(2,1)} async-done(((bf16[4,2,4,16,768]{4,3,2,1,0:T(8,128)(2,1)}), bf16[4,2,4,16,768]{4,3,2,1,0:T(8,128)(2,1)}, u32[]{:S(2)}, u32[]{:S(2)}) %all-to-all-start.4) | async-done | bytes 786464 | tf_op jit(solution)/shard_map/all_to_all | solution.py:40
  121.7 4.1 all-to-all-start.5
  125.9 12.5 %all-to-all-done.5 = bf16[8,2,16,768]{3,2,1,0:T(8,128)(2,1)} async-done(((bf16[8,2,16,768]{3,2,1,0:T(8,128)(2,1)}), bf16[8,2,16,768]{3,2,1,0:T(8,128)(2,1)}, u32[]{:S(2)}, u32[]{:S(2)}) %all-to-all-start.5) | async-done | bytes 393248 | tf_op jit(solution)/shard_map/all_to_all | solution.py:107
  138.4 39.3 %all-gather.6 = s32[32,24,8]{1,2,0:T(8,128)S(1)} all-gather(s32[1,24,8]{1,2,0:T(8,128)S(1)} %bitcast.206), channel_id=2, replica_groups=mesh['dp'=4,'ez'=4,'core'=2] {'dp','ez','core'}, dimensions={0}, use_global_device_ids=true | all-gather | bytes 25344 | tf_op jit(solution)/shard_map/all_gather | solution.py:74
  193.9 37.2 %all-gather.7 = bf16[32,24,8]{1,2,0:T(8,128)(2,1)S(1)} all-gather(bf16[1,24,8]{1,2,0:T(8,128)(2,1)S(1)} %bitcast.207), channel_id=3, replica_groups=mesh['dp'=4,'ez'=4,'core'=2] {'dp','ez','core'}, dimensions={0}, use_global_device_ids=true | all-gather | bytes 12672 | tf_op jit(solution)/shard_map/all_gather | solution.py:74
  237.9 6.6 %all-to-all-done.2 = bf16[8,1,16,768]{3,2,1,0:T(8,128)(2,1)S(1)} async-done(((bf16[8,1,16,768]{3,2,1,0:T(8,128)(2,1)}), bf16[8,1,16,768]{3,2,1,0:T(8,128)(2,1)S(1)}, u32[]{:S(2)}, u32[]{:S(2)}) %all-to-all-start.2) | async-done | bytes 196640 | tf_op jit(solution)/shard_map/all_to_all | solution.py:107
  244.5 12.3 %all-gather.2 = bf16[32,1,16,768]{3,2,1,0:T(8,128)(2,1)S(1)} all-gather(bf16[8,1,16,768]{3,2,1,0:T(8,128)(2,1)S(1)} %all-to-all-done.2), channel_id=4, replica_groups=mesh['dp'=4,'ez'=4,'core'=2] {'dp'}, dimensions={0}, use_global_device_ids=true | all-gather | bytes 983040 | tf_op jit(solution)/shard_map/all_gather | solution.py:108
  269.9 4.5 %bitcast_convert_fusion = bf16[512,768]{1,0:T(8,128)(2,1)} fusion(s32[4,768]{1,0:T(4,128)S(1)} %add_select_fusion, bf16[4,224,512]{2,1,0:T(8,128)(2,1)} %get-tuple-element.21, bf16[4,512,512]{2,1,0:T(8,128)(2,1)} %param.20), kind=kOutput, calls=%fused_computation.25 | convolution fusion | flops 1175945216 | bytes 3813376 | tf_op jit(solution)/shard_map/nr,nt->rt/dot_general | solution.py:17
  279.7 19.2 %all_to_all.89 = bf16[4,8,2,16,768]{4,3,1,2,0:T(8,128)(2,1)} all-to-all(bf16[4,8,2,16,768]{4,3,1,2,0:T(8,128)(2,1)S(1)} %copy_bitcast_fusion), channel_id=1, replica_groups=mesh['dp'=4,'ez'=4,'core'=2] {'dp'}, dimensions={0} | all-to-all | bytes 3145728 | tf_op jit(solution)/shard_map/all_to_all | solution.py:40
  301.4 5.0 %all-to-all-start.7 = ((bf16[8,2,16,768]{3,2,1,0:T(8,128)(2,1)}), bf16[8,2,16,768]{3,2,1,0:T(8,128)(2,1)S(1)}, u32[]{:S(2)}, u32[]{:S(2)}) async-start(bf16[8,2,16,768]{3,2,1,0:T(8,128)(2,1)} %copy.112), calls=%async_computation.7 | async-start | bytes 786432 | tf_op jit(solution)/shard_map/all_to_all | solution.py:143
  306.5 12.5 %all-to-all-done.7 = bf16[8,2,16,768]{3,2,1,0:T(8,128)(2,1)S(1)} async-done(((bf16[8,2,16,768]{3,2,1,0:T(8,128)(2,1)}), bf16[8,2,16,768]{3,2,1,0:T(8,128)(2,1)S(1)}, u32[]{:S(2)}, u32[]{:S(2)}) %all-to-all-start.7) | async-done | bytes 393248 | tf_op jit(solution)/shard_map/all_to_all | solution.py:143
  319.5 10.9 %all-gather.4 = bf16[16,2,16,768]{3,2,1,0:T(8,128)(2,1)S(1)} all-gather(bf16[4,2,16,768]{3,2,1,0:T(8,128)(2,1)S(1)} %select_reduce_fusion.1), channel_id=6, replica_groups=mesh['dp'=4,'ez'=4,'core'=2] {'dp'}, dimensions={0}, use_global_device_ids=true | all-gather | bytes 983040 | tf_op jit(solution)/shard_map/all_gather | solution.py:148
  347.1 10.8 %all-to-all-done.11 = bf16[4,8,1,16,768]{4,3,1,2,0:T(8,128)(2,1)S(1)} async-done(((bf16[4,8,1,16,768]{4,3,1,2,0:T(8,128)(2,1)}), bf16[4,8,1,16,768]{4,3,1,2,0:T(8,128)(2,1)S(1)}, u32[]{:S(2)}, u32[]{:S(2)}) %all-to-all-start.11) | async-done | bytes 786464 | tf_op jit(solution)/shard_map/all_to_all | solution.py:40
  372.1 4.5 %add_convert_fusion = bf16[384,1792]{1,0:T(8,128)(2,1)} fusion(bf16[384,1792]{1,0:T(8,128)(2,1)} %collective-permute-done.2, f32[768,1792]{1,0:T(8,128)} %copy-done.2, pred[]{:T(512)S(6)} %eq.97), kind=kLoop, calls=%fused_computation.9 | loop fusion | flops 2752512 | bytes 8257537 | tf_op jit(solution)/shard_map/convert_element_type | solution.py:169
  383.9 4.3 fusion.25
  392.2 8.7 %all-gather.5 = bf16[16,16,768]{2,1,0:T(8,128)(2,1)S(1)} all-gather(bf16[4,16,768]{2,1,0:T(8,128)(2,1)S(1)} %select_reduce_fusion.3), channel_id=7, replica_groups=mesh['dp'=4,'ez'=4,'core'=2] {'dp'}, dimensions={0}, use_global_device_ids=true | all-gather | bytes 491520 | tf_op jit(solution)/shard_map/all_gather | solution.py:148
  401.0 4.0 fusion.23
  407.1 8.7 %all-to-all-done.8 = bf16[4,96,1792]{2,1,0:T(8,128)(2,1)S(1)} async-done(((bf16[4,96,1792]{2,1,0:T(8,128)(2,1)}), bf16[4,96,1792]{2,1,0:T(8,128)(2,1)S(1)}, u32[]{:S(2)}, u32[]{:S(2)}) %all-to-all-start.8) | async-done | bytes 1376288 | tf_op jit(solution)/shard_map/all_to_all | solution.py:170
  420.3 4.0 fusion.22
  (184 shorter events, 114.9 us)
Async XLA Ops:
  7.2 257.7 %copy-start = (bf16[4,512,512]{2,1,0:T(8,128)(2,1)S(1)}, bf16[4,512,512]{2,1,0:T(8,128)(2,1)}, u32[]{:S(2)}) copy-start(bf16[4,512,512]{2,1,0:T(8,128)(2,1)} %param.21) | copy-start | bytes 6291460
  7.2 46.7 %all-gather.14.cloned.1.call-start = ((), (), s32[]{:S(2)}) async-start(), calls=%async_computation.14 | async-start | bytes 1720320 | tf_op jit(solution)/shard_map/all_gather | solution.py:35
  20.3 67.9 %all-gather.12.cloned.1.call-start = ((), (), s32[]{:S(2)}) async-start(), calls=%async_computation.13 | async-start | bytes 1720320 | tf_op jit(solution)/shard_map/all_gather | solution.py:35
  53.9 34.4 %collective-permute-start.1 = (bf16[384,1792]{1,0:T(8,128)(2,1)}, bf16[384,1792]{1,0:T(8,128)(2,1)S(1)}, u32[]{:S(2)}, u32[]{:S(2)}) collective-permute-start(bf16[384,1792]{1,0:T(8,128)(2,1)} %all-gather.14.cloned.1.call-done), channel_id=1, source_target_pairs={{0,1},{1,0},{2,3},{3,2},{4,5},{5,4},{6,7},{7,6},{8,9},{9,8},{10,11... | collective-permute-start | bytes 4128776 | tf_op jit(solution)/shard_map/ppermute | solution.py:21
  88.2 3.5 collective-permute-start
  100.0 15.7 %all-to-all-start.4 = ((bf16[4,2,4,16,768]{4,3,2,1,0:T(8,128)(2,1)}), bf16[4,2,4,16,768]{4,3,2,1,0:T(8,128)(2,1)}, u32[]{:S(2)}, u32[]{:S(2)}) async-start(bf16[4,2,4,16,768]{4,3,2,1,0:T(8,128)(2,1)} %copy_bitcast_fusion.1), calls=%async_computation.4 | async-start | bytes 1572864 | tf_op jit(solution)/shard_map/all_to_all | solution.py:40
  104.9 33.5 %copy-start.25 = (s32[1024]{0:T(1024)}, s32[1024]{0:T(1024)S(1)}, u32[]{:S(2)}) copy-start(s32[1024]{0:T(1024)S(1)} %pad_clamp_fusion) | copy-start | bytes 12292
  105.0 33.4 %copy-start.23 = (s32[24,8]{0,1:T(8,128)S(1)}, s32[24,8]{0,1:T(8,128)}, u32[]{:S(2)}) copy-start(s32[24,8]{0,1:T(8,128)} %param.13) | copy-start | bytes 2308
  121.7 16.7 %all-to-all-start.5 = ((bf16[8,2,16,768]{3,2,1,0:T(8,128)(2,1)}), bf16[8,2,16,768]{3,2,1,0:T(8,128)(2,1)}, u32[]{:S(2)}, u32[]{:S(2)}) async-start(bf16[8,2,16,768]{3,2,1,0:T(8,128)(2,1)} %broadcast_select_fusion), calls=%async_computation.5 | async-start | bytes 786432 | tf_op jit(solution)/shard_map/all_to_all | solution.py:107
  125.8 132.1 %all-gather.16.cloned.1.call-start = ((), (), s32[]{:S(2)}) async-start(), calls=%async_computation.15 | async-start | bytes 1966080 | tf_op jit(solution)/shard_map/all_gather | solution.py:108
  138.4 41.7 %copy-start.28 = (s32[4]{0:T(128)}, s32[4]{0:T(128)S(1)}, u32[]{:S(2)}) copy-start(s32[4]{0:T(128)S(1)} %iota_add_fusion) | copy-start | bytes 52
  189.5 41.8 %copy-start.24 = (pred[4,768]{1,0:T(4,128)(4,1)S(1)}, pred[4,768]{1,0:T(4,128)(4,1)}, u32[]{:S(2)}) copy-start(pred[4,768]{1,0:T(4,128)(4,1)} %reduce_or.12) | copy-start | bytes 9220
  189.5 42.6 %copy-start.27 = (pred[8]{0:T(512)(128)(4,1)S(1)}, pred[8]{0:T(512)(128)(4,1)}, u32[]{:S(2)}) copy-start(pred[8]{0:T(512)(128)(4,1)} %copy-done.26) | copy-start | bytes 28
  189.5 46.8 %copy-start.19 = (s32[32,24,8]{0,2,1:T(8,128)S(1)}, s32[32,24,8]{0,2,1:T(8,128)}, u32[]{:S(2)}) copy-start(s32[32,24,8]{0,2,1:T(8,128)} %copy.97) | copy-start | bytes 73732
  189.5 46.8 %copy-start.29 = (s32[4]{0:T(128)S(1)}, s32[4]{0:T(128)}, u32[]{:S(2)}) copy-start(s32[4]{0:T(128)} %copy-done.28) | copy-start | bytes 52
  190.3 41.0 %all-to-all-start.1 = ((bf16[4,1,4,16,768]{4,3,2,1,0:T(8,128)(2,1)}), bf16[4,1,4,16,768]{4,3,2,1,0:T(8,128)(2,1)S(1)}, u32[]{:S(2)}, u32[]{:S(2)}) async-start(bf16[4,1,4,16,768]{4,3,2,1,0:T(8,128)(2,1)} %bitcast.152), calls=%async_computation.1 | async-start | bytes 786432 | tf_op jit(solution)/shard_map/all_to_all | solution.py:40
  232.9 11.7 %all-to-all-start.2 = ((bf16[8,1,16,768]{3,2,1,0:T(8,128)(2,1)}), bf16[8,1,16,768]{3,2,1,0:T(8,128)(2,1)S(1)}, u32[]{:S(2)}, u32[]{:S(2)}) async-start(bf16[8,1,16,768]{3,2,1,0:T(8,128)(2,1)} %bitcast_select_fusion), calls=%async_computation.2 | async-start | bytes 393216 | tf_op jit(solution)/shard_map/all_to_all | solution.py:107
  301.4 17.6 %all-to-all-start.7 = ((bf16[8,2,16,768]{3,2,1,0:T(8,128)(2,1)}), bf16[8,2,16,768]{3,2,1,0:T(8,128)(2,1)S(1)}, u32[]{:S(2)}, u32[]{:S(2)}) async-start(bf16[8,2,16,768]{3,2,1,0:T(8,128)(2,1)} %copy.112), calls=%async_computation.7 | async-start | bytes 786432 | tf_op jit(solution)/shard_map/all_to_all | solution.py:143
  336.3 35.7 %collective-permute-start.2 = (bf16[384,1792]{1,0:T(8,128)(2,1)}, bf16[384,1792]{1,0:T(8,128)(2,1)}, u32[]{:S(2)}, u32[]{:S(2)}) collective-permute-start(bf16[384,1792]{1,0:T(8,128)(2,1)} %select_convert_fusion.1), channel_id=1, source_target_pairs={{0,1},{1,0},{2,3},{3,2},{4,5},{5,4},{6,7},{7,6},{8,9},{9,8},{10,11... | collective-permute-start | bytes 4128776 | tf_op jit(solution)/shard_map/ppermute | solution.py:21
  342.7 15.2 %all-to-all-start.11 = ((bf16[4,8,1,16,768]{4,3,1,2,0:T(8,128)(2,1)}), bf16[4,8,1,16,768]{4,3,1,2,0:T(8,128)(2,1)S(1)}, u32[]{:S(2)}, u32[]{:S(2)}) async-start(bf16[4,8,1,16,768]{4,3,1,2,0:T(8,128)(2,1)} %copy.122), calls=%async_computation.11 | async-start | bytes 1572864 | tf_op jit(solution)/shard_map/all_to_all | solution.py:40
  357.9 10.7 %all-to-all-start.10 = ((f32[32,4,24]{2,1,0:T(4,128)}), f32[32,4,24]{2,1,0:T(4,128)S(1)}, u32[]{:S(2)}, u32[]{:S(2)}) async-start(f32[32,4,24]{2,1,0:T(4,128)} %copy.117), calls=%async_computation.10 | async-start | bytes 131072 | tf_op jit(solution)/shard_map/all_to_all | solution.py:180
  368.7 11.7 %all-to-all-start.12 = ((bf16[8,1,16,768]{3,2,1,0:T(8,128)(2,1)}), bf16[8,1,16,768]{3,2,1,0:T(8,128)(2,1)S(1)}, u32[]{:S(2)}, u32[]{:S(2)}) async-start(bf16[8,1,16,768]{3,2,1,0:T(8,128)(2,1)} %bitcast.75), calls=%async_computation.12 | async-start | bytes 393216 | tf_op jit(solution)/shard_map/all_to_all | solution.py:143
  380.3 35.5 %all-to-all-start.8 = ((bf16[4,96,1792]{2,1,0:T(8,128)(2,1)}), bf16[4,96,1792]{2,1,0:T(8,128)(2,1)S(1)}, u32[]{:S(2)}, u32[]{:S(2)}) async-start(bf16[4,96,1792]{2,1,0:T(8,128)(2,1)} %bitcast.52), calls=%async_computation.8 | async-start | bytes 2752512 | tf_op jit(solution)/shard_map/all_to_all | solution.py:170
  416.8 9.0 %all-to-all-start.9 = ((bf16[4,24,1792]{2,1,0:T(8,128)(2,1)}), bf16[4,24,1792]{2,1,0:T(8,128)(2,1)S(1)}, u32[]{:S(2)}, u32[]{:S(2)}) async-start(bf16[4,24,1792]{2,1,0:T(8,128)(2,1)} %bitcast.53), calls=%async_computation.9 | async-start | bytes 688128 | tf_op jit(solution)/shard_map/all_to_all | solution.py:172
  (27 other events, 151.9 us)
Sparse Core Ops, SparseCore 0:
  20.4 33.3 all-gather.13
  55.4 32.7 all-gather.11
  138.5 29.1 all-gather.15
